TPU v7x, 512 devices: a whole 4x8x8 slice. The times are simulated.
512 devices in a mesh: tm: 128 (over z, y, core), swath: 4 (over x).
Axes of the slice: x: 4, y: 8, z: 8, core: 2. Of those that a mesh axis runs over, the one named last changes fastest.
Arguments:
- design: bfloat16 [128, 2048, 512], P('tm', 'swath'), may hold values from -6 to 6
- process: bfloat16 [128, 512, 512], P('tm', 'swath')
- prior_prec: float32 [128, 512], P('tm', 'swath'), may hold values from 0.05 to 0.5
- routes: int32 [128, 16], P('tm', 'swath'), may hold values from -1 to 127, as said below
- counts: int32 [128, 4], P('tm', 'swath'), may hold values from 1 to 4
Outputs:
- reduced_diag: float32 [128, 512, 512], P('tm', 'swath')
- reduced_coupling: float32 [128, 512, 512], P('tm', 'swath')
Inputs may be any that keep to these rules, and one draw needn't show every extreme that they name: `routes`: each value is the holder's own time block i or i + 1, or -1 only where i + 1 would be 128; of one holder's 4 blocks, exactly 2 name i and the others i + 1 or -1.
All inputs are finite; a program needn't handle non-finite values.
Results may differ from a plain program's by a relative error of at most 0.00073.
Values may be sent and summed in bfloat16 or wider, within the bound.
No kernel may reach another device: no remote copies, remote signals or barrier semaphores. Data moves between devices by JAX's collectives and lax.ppermute only.
A program may use at most 64 MiB of HBM per device.

v0:
```python
import jax
import jax.numpy as jnp
from jax import lax
from jax.sharding import PartitionSpec as P

LEVELS = 3


def passed_along(block, axis, distance):
    devices = range(lax.axis_size(axis))
    route = [(i - distance, i) for i in devices if i - distance in devices]
    return lax.ppermute(block, axis, route)


def tri_solve(factor, right):
    return lax.linalg.triangular_solve(factor, right, left_side=True, lower=True)


def inner_rows(left_side, right_side):
    return lax.dot_general(
        left_side,
        right_side,
        (((0,), (0,)), ((), ())),
        precision=lax.Precision.HIGHEST,
        preferred_element_type=jnp.float32,
    )


def compact(scaled, wanted, slot_count):
    sort_key = jnp.where(wanted, 0, 1).astype(jnp.int32)
    picked = jnp.argsort(sort_key, stable=True)[:slot_count]
    kept = jnp.take(sort_key, picked) == 0
    return jnp.where(kept[:, None, None], scaled[picked], 0.0).astype(jnp.bfloat16)


def shards(design, process, prior_prec, routes, counts):
    row_count = process.shape[1]
    order_size = process.shape[2]
    time_count = lax.axis_size("tm")
    my_time = lax.axis_index("tm")
    swath_index = lax.axis_index("swath")
    block_count = routes.shape[1]
    slot_count = block_count // 2
    block_rows = design.shape[1] // block_count
    total_slots = 2 * slot_count * block_rows * lax.axis_size("swath")
    row_start = swath_index * row_count
    raw_rows = design[0].reshape(block_count, block_rows, order_size).astype(jnp.float32)
    mean_sq = jnp.mean(raw_rows * raw_rows, axis=-1, keepdims=True)
    scaled = raw_rows * lax.rsqrt(4.0 * total_slots * (mean_sq + 1e-06))
    live = jnp.arange(block_count) < counts[0, 0]
    target = routes[0]
    own_blocks = compact(scaled, live & (target == my_time), slot_count)
    ahead_blocks = compact(scaled, live & (target == my_time + 1), slot_count)
    incoming, previous = passed_along((ahead_blocks, process), "tm", 1)
    gram_input = jnp.concatenate([own_blocks, incoming], axis=0).reshape(-1, order_size)
    shard_rows = lax.all_gather(gram_input, "swath", axis=0, tiled=True)
    columns = lax.dynamic_slice_in_dim(shard_rows, row_start, row_count, 1)
    gram = lax.dot_general(
        columns, shard_rows, (((0,), (0,)), ((), ())), preferred_element_type=jnp.float32
    )
    unit_rows = jnp.arange(order_size)[None, :] == jnp.arange(row_count)[:, None] + row_start
    diag_rows = previous[0].astype(jnp.float32) + process[0].astype(jnp.float32) + gram
    diag_rows = diag_rows + jnp.where(unit_rows, prior_prec[0][:, None], 0.0)
    coup_rows = -process[0].astype(jnp.float32)
    unit_full = jnp.eye(order_size, dtype=jnp.float32)
    for level in range(LEVELS):
        distance = 2**level
        full_diag, full_coup = (
            lax.all_gather(diag_rows, "swath", axis=0, tiled=True),
            lax.all_gather(coup_rows, "swath", axis=0, tiled=True),
        )
        factor = jnp.linalg.cholesky(full_diag)
        solved = tri_solve(factor, full_coup)
        own_cols = lax.dynamic_slice_in_dim(solved, row_start, row_count, 1)
        eliminated = inner_rows(own_cols, solved)
        left_term = passed_along(eliminated, "tm", distance)
        far_factor, far_solved = passed_along((factor, solved), "tm", -distance)
        has_partner = my_time + distance < time_count
        far_factor = jnp.where(has_partner, far_factor, unit_full)
        cross = tri_solve(far_factor, full_coup.T)
        cross_cols = lax.dynamic_slice_in_dim(cross, row_start, row_count, 1)
        right_term = inner_rows(cross_cols, cross)
        new_coupling = inner_rows(cross_cols, far_solved)
        diag_rows = diag_rows - left_term - jnp.where(has_partner, right_term, 0.0)
        coup_rows = -new_coupling
    return (diag_rows[None], coup_rows[None])


def solution(mesh):
    return jax.shard_map(
        shards,
        mesh=mesh,
        in_specs=(
            P("tm", "swath", None),
            P("tm", "swath", None),
            P("tm", "swath"),
            P("tm", "swath"),
            P("tm", "swath"),
        ),
        out_specs=(P("tm", "swath", None), P("tm", "swath", None)),
        check_vma=False,
    )
```

profile of v0, /device:TPU:16, one launch (start us, length us, event | category | flops | bytes accessed | tf_op | source)
XLA Modules:
  0.0 882.1 jit_solution(11233047935860242572)
XLA Ops:
  17.1 4.4 collective-permute-done.1
  24.6 4.3 collective-permute-done
  28.9 35.5 %all-gather.9.cloned.1.call-done = bf16[2048,512]{1,0:T(8,128)(2,1)} async-done(((bf16[512,512]{1,0:T(8,128)(2,1)}), bf16[2048,512]{1,0:T(8,128)(2,1)}) %all-gather.9.cloned.1.call-update) | async-done | bytes 2097168 | tf_op jit(solution)/shard_map/all_gather | solution.py:56
  64.4 3.3 fusion.71
  68.6 30.6 %all-gather.11.cloned.1.call-done = f32[512,512]{0,1:T(8,128)} async-done(((f32[128,512]{0,1:T(8,128)}), f32[512,512]{0,1:T(8,128)}) %all-gather.11.cloned.1.call-update) | async-done | bytes 1048592 | tf_op jit(solution)/shard_map/all_gather | solution.py:69
  101.1 11.7 %cholesky.374 = f32[128,128]{1,0:T(8,128)S(1)} custom-call(f32[128,128]{1,0:T(8,128)S(1)} %cholesky.586), custom_call_target="Cholesky" | custom-call | tf_op jit(solution)/shard_map/jit(cholesky)/cholesky | solution.py:72
  113.0 9.8 %custom-call.34 = f32[1,128,128]{1,2,0:T(8,128)S(1)} custom-call(f32[1,128,128]{2,1,0:T(8,128)S(1)} %get-tuple-element.152), custom_call_target="InvertDiagBlocksLowerTriangular" | custom-call | tf_op jit(solution)/shard_map/jit(cholesky)/cholesky | solution.py:72
  123.5 11.7 %cholesky.393 = f32[128,128]{1,0:T(8,128)S(1)} custom-call(f32[128,128]{1,0:T(8,128)S(1)} %cholesky.590), custom_call_target="Cholesky" | custom-call | tf_op jit(solution)/shard_map/jit(cholesky)/cholesky | solution.py:72
  135.2 10.2 %custom-call.35 = f32[1,128,128]{1,2,0:T(8,128)S(1)} custom-call(f32[1,128,128]{2,1,0:T(8,128)S(1)} %get-tuple-element.149), custom_call_target="InvertDiagBlocksLowerTriangular" | custom-call | tf_op jit(solution)/shard_map/jit(cholesky)/cholesky | solution.py:72
  146.1 11.7 %cholesky.414 = f32[128,128]{1,0:T(8,128)S(1)} custom-call(f32[128,128]{1,0:T(8,128)S(1)} %cholesky.595), custom_call_target="Cholesky" | custom-call | tf_op jit(solution)/shard_map/jit(cholesky)/cholesky | solution.py:72
  157.9 9.8 %custom-call.36 = f32[1,128,128]{1,2,0:T(8,128)S(1)} custom-call(f32[1,128,128]{2,1,0:T(8,128)S(1)} %get-tuple-element.146), custom_call_target="InvertDiagBlocksLowerTriangular" | custom-call | tf_op jit(solution)/shard_map/jit(cholesky)/cholesky | solution.py:72
  168.3 11.7 %cholesky.431 = f32[128,128]{1,0:T(8,128)S(1)} custom-call(f32[128,128]{1,0:T(8,128)S(1)} %convolution_subtract_fusion.14), custom_call_target="Cholesky" | custom-call | tf_op jit(solution)/shard_map/jit(cholesky)/cholesky | solution.py:72
  185.5 7.5 while.12
  193.0 39.3 %custom-call.37 = f32[4,128,128]{1,2,0:T(8,128)S(1)} custom-call(f32[4,128,128]{2,1,0:T(8,128)S(1)} %get-tuple-element.47), custom_call_target="InvertDiagBlocksLowerTriangular" | custom-call | tf_op jit(solution)/shard_map/triangular_solve/custom-call.3 | solution.py:16
  241.2 2.5 fusion.103
  243.7 2.4 collective-permute-start.2
  246.1 5.0 collective-permute-done.3
  251.9 10.2 %while.13 = (s32[]{:T(128)}, f32[512,512]{1,0:T(8,128)S(1)}, s32[4,2]{0,1:T(2,128)S(1)}, f32[4,128,128]{2,1,0:T(8,128)}, s32[]{:T(128)}) while((s32[]{:T(128)}, f32[512,512]{1,0:T(8,128)S(1)}, s32[4,2]{0,1:T(2,128)S(1)}, f32[4,128,128]{2,1,0:T(8,128)}, s32[]{:T(128)}) %tuple.157), condition=%wide.while_cond.clone, body=%wide.while_body.clone.sunk | while | flops 2 | bytes 132205 | solution.py:16
  252.6 1.9 bitcast_dynamic-update-slice_fusion.13
  262.2 40.7 %custom-call.38 = f32[4,128,128]{1,2,0:T(8,128)} custom-call(f32[4,128,128]{2,1,0:T(8,128)} %get-tuple-element.48), custom_call_target="InvertDiagBlocksLowerTriangular" | custom-call | tf_op jit(solution)/shard_map/triangular_solve/custom-call.3 | solution.py:16
  308.0 2.5 subtract_subtract_fusion.1
  310.6 3.8 collective-permute-start.4
  314.4 12.3 %collective-permute-done.4 = f32[512,512]{1,0:T(8,128)S(1)} collective-permute-done((f32[512,512]{1,0:T(8,128)S(1)}, f32[512,512]{1,0:T(8,128)S(1)}, u32[]{:S(2)}, u32[]{:S(2)}) %collective-permute-start.4) | collective-permute-done | bytes 1048608 | tf_op jit(solution)/shard_map/ppermute | solution.py:12
  328.6 15.1 %all-gather.13.cloned.1.call-done = f32[512,512]{0,1:T(8,128)} async-done(((f32[128,512]{0,1:T(8,128)}), f32[512,512]{0,1:T(8,128)}) %all-gather.13.cloned.1.call-update) | async-done | bytes 1048592 | tf_op jit(solution)/shard_map/all_gather | solution.py:69
  345.6 11.7 %cholesky.446 = f32[128,128]{1,0:T(8,128)S(1)} custom-call(f32[128,128]{1,0:T(8,128)S(1)} %cholesky.599), custom_call_target="Cholesky" | custom-call | tf_op jit(solution)/shard_map/jit(cholesky)/cholesky | solution.py:72
  357.5 9.8 %custom-call.39 = f32[1,128,128]{1,2,0:T(8,128)S(1)} custom-call(f32[1,128,128]{2,1,0:T(8,128)S(1)} %get-tuple-element.142), custom_call_target="InvertDiagBlocksLowerTriangular" | custom-call | tf_op jit(solution)/shard_map/jit(cholesky)/cholesky | solution.py:72
  368.0 11.7 %cholesky.465 = f32[128,128]{1,0:T(8,128)S(1)} custom-call(f32[128,128]{1,0:T(8,128)S(1)} %cholesky.603), custom_call_target="Cholesky" | custom-call | tf_op jit(solution)/shard_map/jit(cholesky)/cholesky | solution.py:72
  379.7 10.0 %custom-call.40 = f32[1,128,128]{1,2,0:T(8,128)S(1)} custom-call(f32[1,128,128]{2,1,0:T(8,128)S(1)} %get-tuple-element.139), custom_call_target="InvertDiagBlocksLowerTriangular" | custom-call | tf_op jit(solution)/shard_map/jit(cholesky)/cholesky | solution.py:72
  390.4 11.7 %cholesky.486 = f32[128,128]{1,0:T(8,128)S(1)} custom-call(f32[128,128]{1,0:T(8,128)S(1)} %cholesky.608), custom_call_target="Cholesky" | custom-call | tf_op jit(solution)/shard_map/jit(cholesky)/cholesky | solution.py:72
  402.1 9.8 %custom-call.41 = f32[1,128,128]{1,2,0:T(8,128)S(1)} custom-call(f32[1,128,128]{2,1,0:T(8,128)S(1)} %get-tuple-element.136), custom_call_target="InvertDiagBlocksLowerTriangular" | custom-call | tf_op jit(solution)/shard_map/jit(cholesky)/cholesky | solution.py:72
  412.5 11.7 %cholesky.503 = f32[128,128]{1,0:T(8,128)S(1)} custom-call(f32[128,128]{1,0:T(8,128)S(1)} %convolution_subtract_fusion.13), custom_call_target="Cholesky" | custom-call | tf_op jit(solution)/shard_map/jit(cholesky)/cholesky | solution.py:72
  429.7 7.5 while.14
  437.3 39.3 %custom-call.42 = f32[4,128,128]{1,2,0:T(8,128)S(1)} custom-call(f32[4,128,128]{2,1,0:T(8,128)S(1)} %get-tuple-element.49), custom_call_target="InvertDiagBlocksLowerTriangular" | custom-call | tf_op jit(solution)/shard_map/triangular_solve/custom-call.3 | solution.py:16
  480.3 2.4 collective-permute-start.6
  484.4 2.5 fusion.101
  486.9 3.8 collective-permute-start.5
  490.7 15.6 %collective-permute-done.6 = f32[512,512]{1,0:T(8,128)S(1)} collective-permute-done((f32[512,512]{1,0:T(8,128)S(1)}, f32[512,512]{1,0:T(8,128)S(1)}, u32[]{:S(2)}, u32[]{:S(2)}) %collective-permute-start.6) | collective-permute-done | bytes 1048608 | tf_op jit(solution)/shard_map/ppermute | solution.py:12
  507.1 10.2 %while.15 = (s32[]{:T(128)}, f32[512,512]{1,0:T(8,128)S(1)}, s32[4,2]{0,1:T(2,128)S(1)}, f32[4,128,128]{2,1,0:T(8,128)}, s32[]{:T(128)}) while((s32[]{:T(128)}, f32[512,512]{1,0:T(8,128)S(1)}, s32[4,2]{0,1:T(2,128)S(1)}, f32[4,128,128]{2,1,0:T(8,128)}, s32[]{:T(128)}) %tuple.159), condition=%wide.while_cond.clone.2, body=%wide.while_body.clone.2.sunk | while | flops 2 | bytes 132205 | solution.py:16
  512.8 1.9 bitcast_dynamic-update-slice_fusion.15
  517.3 40.7 %custom-call.43 = f32[4,128,128]{1,2,0:T(8,128)} custom-call(f32[4,128,128]{2,1,0:T(8,128)} %get-tuple-element.50), custom_call_target="InvertDiagBlocksLowerTriangular" | custom-call | tf_op jit(solution)/shard_map/triangular_solve/custom-call.3 | solution.py:16
  564.8 2.5 subtract_subtract_fusion
  567.4 2.6 collective-permute-start.7
  570.0 23.3 %collective-permute-done.7 = f32[512,512]{1,0:T(8,128)S(1)} collective-permute-done((f32[512,512]{1,0:T(8,128)S(1)}, f32[512,512]{1,0:T(8,128)S(1)}, u32[]{:S(2)}, u32[]{:S(2)}) %collective-permute-start.7) | collective-permute-done | bytes 1048608 | tf_op jit(solution)/shard_map/ppermute | solution.py:12
  594.9 4.9 all-gather.17.cloned.1.call-done
  601.6 11.7 %cholesky.518 = f32[128,128]{1,0:T(8,128)S(1)} custom-call(f32[128,128]{1,0:T(8,128)S(1)} %cholesky.612), custom_call_target="Cholesky" | custom-call | tf_op jit(solution)/shard_map/jit(cholesky)/cholesky | solution.py:72
  613.5 9.8 %custom-call.44 = f32[1,128,128]{1,2,0:T(8,128)S(1)} custom-call(f32[1,128,128]{2,1,0:T(8,128)S(1)} %get-tuple-element.132), custom_call_target="InvertDiagBlocksLowerTriangular" | custom-call | tf_op jit(solution)/shard_map/jit(cholesky)/cholesky | solution.py:72
  624.0 11.7 %cholesky.537 = f32[128,128]{1,0:T(8,128)S(1)} custom-call(f32[128,128]{1,0:T(8,128)S(1)} %cholesky.616), custom_call_target="Cholesky" | custom-call | tf_op jit(solution)/shard_map/jit(cholesky)/cholesky | solution.py:72
  635.8 10.0 %custom-call.45 = f32[1,128,128]{1,2,0:T(8,128)S(1)} custom-call(f32[1,128,128]{2,1,0:T(8,128)S(1)} %get-tuple-element.129), custom_call_target="InvertDiagBlocksLowerTriangular" | custom-call | tf_op jit(solution)/shard_map/jit(cholesky)/cholesky | solution.py:72
  646.4 11.7 %cholesky.558 = f32[128,128]{1,0:T(8,128)S(1)} custom-call(f32[128,128]{1,0:T(8,128)S(1)} %cholesky.621), custom_call_target="Cholesky" | custom-call | tf_op jit(solution)/shard_map/jit(cholesky)/cholesky | solution.py:72
  658.2 9.8 %custom-call.46 = f32[1,128,128]{1,2,0:T(8,128)S(1)} custom-call(f32[1,128,128]{2,1,0:T(8,128)S(1)} %get-tuple-element.126), custom_call_target="InvertDiagBlocksLowerTriangular" | custom-call | tf_op jit(solution)/shard_map/jit(cholesky)/cholesky | solution.py:72
  668.6 12.1 %cholesky.575 = f32[128,128]{1,0:T(8,128)S(1)} custom-call(f32[128,128]{1,0:T(8,128)S(1)} %convolution_subtract_fusion.12), custom_call_target="Cholesky" | custom-call | tf_op jit(solution)/shard_map/jit(cholesky)/cholesky | solution.py:72
  686.0 7.9 while.16
  693.9 39.3 %custom-call.47 = f32[4,128,128]{1,2,0:T(8,128)S(1)} custom-call(f32[4,128,128]{2,1,0:T(8,128)S(1)} %get-tuple-element.51), custom_call_target="InvertDiagBlocksLowerTriangular" | custom-call | tf_op jit(solution)/shard_map/triangular_solve/custom-call.3 | solution.py:16
  736.9 2.4 collective-permute-start.9
  742.9 2.5 fusion.99
  745.4 6.2 collective-permute-start.8
  751.6 59.3 %collective-permute-done.9 = f32[512,512]{1,0:T(8,128)S(1)} collective-permute-done((f32[512,512]{1,0:T(8,128)S(1)}, f32[512,512]{1,0:T(8,128)S(1)}, u32[]{:S(2)}, u32[]{:S(2)}) %collective-permute-start.9) | collective-permute-done | bytes 1048608 | tf_op jit(solution)/shard_map/ppermute | solution.py:12
  811.8 10.4 %while.17 = (s32[]{:T(128)}, f32[512,512]{1,0:T(8,128)S(1)}, s32[4,2]{0,1:T(2,128)S(1)}, f32[4,128,128]{2,1,0:T(8,128)}, s32[]{:T(128)}) while((s32[]{:T(128)}, f32[512,512]{1,0:T(8,128)S(1)}, s32[4,2]{0,1:T(2,128)S(1)}, f32[4,128,128]{2,1,0:T(8,128)}, s32[]{:T(128)}) %tuple.161), condition=%wide.while_cond.clone.4, body=%wide.while_body.clone.4.sunk | while | flops 2 | bytes 132205 | solution.py:16
  812.4 2.0 bitcast_dynamic-update-slice_fusion.17
  815.0 2.0 bitcast_dynamic-update-slice_fusion.17
  817.6 2.0 bitcast_dynamic-update-slice_fusion.17
  820.2 2.0 bitcast_dynamic-update-slice_fusion.17
  822.2 40.7 %custom-call.48 = f32[4,128,128]{1,2,0:T(8,128)} custom-call(f32[4,128,128]{2,1,0:T(8,128)} %get-tuple-element.52), custom_call_target="InvertDiagBlocksLowerTriangular" | custom-call | tf_op jit(solution)/shard_map/triangular_solve/custom-call.3 | solution.py:16
  872.3 2.7 fusion
  (268 shorter events, 123.9 us)
Async XLA Ops:
  7.2 57.3 %all-gather.9.cloned.1.call-start = ((), (), s32[]{:S(2)}) async-start(), calls=%async_computation | async-start | bytes 2621440 | tf_op jit(solution)/shard_map/all_gather | solution.py:56
  13.1 9.3 %copy-start.12 = (bf16[1,128,512]{2,1,0:T(8,128)(2,1)S(1)}, bf16[1,128,512]{2,1,0:T(8,128)(2,1)}, u32[]{:S(2)}) copy-start(bf16[1,128,512]{2,1,0:T(8,128)(2,1)} %param.11) | copy-start | bytes 393220
  13.7 50.7 %copy-start.13 = (f32[1,128]{1,0:T(1,128)S(1)}, f32[1,128]{1,0:T(1,128)}, u32[]{:S(2)}) copy-start(f32[1,128]{1,0:T(1,128)} %param.12) | copy-start | bytes 1540
  13.9 7.7 collective-permute-start.1
  22.4 76.8 %all-gather.11.cloned.1.call-start = ((), (), s32[]{:S(2)}) async-start(), calls=%async_computation.1 | async-start | bytes 1310720 | tf_op jit(solution)/shard_map/all_gather | solution.py:69
  22.6 6.3 collective-permute-start
  67.8 164.6 %all-gather.21.cloned.1.call-start = ((), (), s32[]{:S(2)}) async-start(), calls=%async_computation.6 | async-start | bytes 1310720 | tf_op jit(solution)/shard_map/all_gather | solution.py:70
  68.6 275.1 %all-gather.13.cloned.1.call-start = ((), (), s32[]{:S(2)}) async-start(), calls=%async_computation.2 | async-start | bytes 1310720 | tf_op jit(solution)/shard_map/all_gather | solution.py:69
  99.2 1.7 copy-start.4
  232.4 3.5 copy-start.5
  236.9 14.2 %collective-permute-start.3 = (f32[512,512]{1,0:T(8,128)S(1)}, f32[512,512]{1,0:T(8,128)S(1)}, u32[]{:S(2)}, u32[]{:S(2)}) collective-permute-start(f32[512,512]{1,0:T(8,128)S(1)} %get-tuple-element.110), channel_id=1, source_target_pairs={{4,0},{8,4},{12,8},{16,12},{20,16},{24,20},{28,24},{32,28},{36,32}... | collective-permute-start | bytes 3145736 | tf_op jit(solution)/shard_map/ppermute | solution.py:12
  243.7 64.2 %collective-permute-start.2 = (f32[128,512]{0,1:T(8,128)}, f32[128,512]{0,1:T(8,128)S(1)}, u32[]{:S(2)}, u32[]{:S(2)}) collective-permute-start(f32[128,512]{0,1:T(8,128)} %fusion.103), channel_id=1, source_target_pairs={{0,4},{4,8},{8,12},{12,16},{16,20},{20,24},{24,28},{28,32},{32,36}... | collective-permute-start | bytes 786440 | tf_op jit(solution)/shard_map/ppermute | solution.py:12
  302.9 3.4 copy-start.9
  306.8 1.2 copy-start.8
  310.5 166.1 %all-gather.15.cloned.1.call-start = ((), (), s32[]{:S(2)}) async-start(), calls=%async_computation.3 | async-start | bytes 1310720 | tf_op jit(solution)/shard_map/all_gather | solution.py:70
  310.6 16.1 %collective-permute-start.4 = (f32[512,512]{1,0:T(8,128)S(1)}, f32[512,512]{1,0:T(8,128)S(1)}, u32[]{:S(2)}, u32[]{:S(2)}) collective-permute-start(f32[512,512]{1,0:T(8,128)S(1)} %pad_maximum_fusion), channel_id=1, source_target_pairs={{4,0},{8,4},{12,8},{16,12},{20,16},{24,20},{28,24},{32,28},{36,32}... | collective-permute-start | bytes 3145736 | tf_op jit(solution)/shard_map/ppermute | solution.py:12
  328.2 271.6 %all-gather.17.cloned.1.call-start = ((), (), s32[]{:S(2)}) async-start(), calls=%async_computation.4 | async-start | bytes 1310720 | tf_op jit(solution)/shard_map/all_gather | solution.py:69
  343.7 1.7 copy-start.2
  476.6 6.1 copy-start.1
  480.3 25.9 %collective-permute-start.6 = (f32[512,512]{1,0:T(8,128)S(1)}, f32[512,512]{1,0:T(8,128)S(1)}, u32[]{:S(2)}, u32[]{:S(2)}) collective-permute-start(f32[512,512]{1,0:T(8,128)S(1)} %get-tuple-element.108), channel_id=1, source_target_pairs={{8,0},{12,4},{16,8},{20,12},{24,16},{28,20},{32,24},{36,28},{40,32... | collective-permute-start | bytes 3145736 | tf_op jit(solution)/shard_map/ppermute | solution.py:12
  486.9 77.9 %collective-permute-start.5 = (f32[128,512]{0,1:T(8,128)}, f32[128,512]{0,1:T(8,128)S(1)}, u32[]{:S(2)}, u32[]{:S(2)}) collective-permute-start(f32[128,512]{0,1:T(8,128)} %fusion.101), channel_id=1, source_target_pairs={{0,8},{4,12},{8,16},{12,20},{16,24},{20,28},{24,32},{28,36},{32,40... | collective-permute-start | bytes 786440 | tf_op jit(solution)/shard_map/ppermute | solution.py:12
  558.1 4.2 copy-start.10
  562.7 2.0 copy-start.7
  567.3 165.9 %all-gather.19.cloned.1.call-start = ((), (), s32[]{:S(2)}) async-start(), calls=%async_computation.5 | async-start | bytes 1310720 | tf_op jit(solution)/shard_map/all_gather | solution.py:70
  567.4 26.0 %collective-permute-start.7 = (f32[512,512]{1,0:T(8,128)S(1)}, f32[512,512]{1,0:T(8,128)S(1)}, u32[]{:S(2)}, u32[]{:S(2)}) collective-permute-start(f32[512,512]{1,0:T(8,128)S(1)} %pad_maximum_fusion.2), channel_id=1, source_target_pairs={{8,0},{12,4},{16,8},{20,12},{24,16},{28,20},{32,24},{36,28},{40,32... | collective-permute-start | bytes 3145736 | tf_op jit(solution)/shard_map/ppermute | solution.py:12
  599.7 1.7 copy-start.3
  733.2 6.1 copy-start
  736.9 74.0 %collective-permute-start.9 = (f32[512,512]{1,0:T(8,128)S(1)}, f32[512,512]{1,0:T(8,128)S(1)}, u32[]{:S(2)}, u32[]{:S(2)}) collective-permute-start(f32[512,512]{1,0:T(8,128)S(1)} %get-tuple-element.106), channel_id=1, source_target_pairs={{16,0},{20,4},{24,8},{28,12},{32,16},{36,20},{40,24},{44,28},{48,3... | collective-permute-start | bytes 3145736 | tf_op jit(solution)/shard_map/ppermute | solution.py:12
  740.9 131.4 %collective-permute-start.10 = (f32[512,512]{1,0:T(8,128)S(1)}, f32[512,512]{1,0:T(8,128)}, u32[]{:S(2)}, u32[]{:S(2)}) collective-permute-start(f32[512,512]{1,0:T(8,128)S(1)} %pad_maximum_fusion.4), channel_id=1, source_target_pairs={{16,0},{20,4},{24,8},{28,12},{32,16},{36,20},{40,24},{44,28},{48,3... | collective-permute-start | bytes 3145736 | tf_op jit(solution)/shard_map/ppermute | solution.py:12
  745.4 124.3 %collective-permute-start.8 = (f32[128,512]{0,1:T(8,128)}, f32[128,512]{0,1:T(8,128)S(1)}, u32[]{:S(2)}, u32[]{:S(2)}) collective-permute-start(f32[128,512]{0,1:T(8,128)} %fusion.99), channel_id=1, source_target_pairs={{0,16},{4,20},{8,24},{12,28},{16,32},{20,36},{24,40},{28,44},{32,4... | collective-permute-start | bytes 786440 | tf_op jit(solution)/shard_map/ppermute | solution.py:12
  862.9 4.2 copy-start.11
  867.6 2.0 copy-start.6
Sparse Core Ops, SparseCore 0:
  22.5 41.8 all-gather.8
  67.9 31.2 all-gather.10
  101.9 32.4 all-gather.20
  310.6 33.0 all-gather.12
  346.2 30.5 all-gather.14
  567.5 32.2 all-gather.16
  602.4 30.6 all-gather.18
where the time goes:
time: 894 us; the launch traced here: 882 us
  other arithmetic  487 us (54%)
  waiting for transfers between devices  210 us (23%)
  local copies, waits for them, and re-layouts  64.4 us (7%)
  matrix products  64 us (7%)
  starting transfers between devices  32.1 us (4%)
  between operations  23.4 us (3%)
    another operation x19, other arithmetic, tri_solve(): lax.linalg.triangular_solve(factor, right, left_side=True, lower=True)  242 us
    another operation x45, other arithmetic, shards(): factor = jnp.linalg.cholesky(full_diag)  238 us
    ppermute x11, waiting for transfers between devices, passed_along(): return lax.ppermute(block, axis, route)  124 us
    another operation x79, local copies, waits for them, and re-layouts, tri_solve(): lax.linalg.triangular_solve(factor, right, left_side=True, lower=True)  55.7 us
    all_gather x3, waiting for transfers between devices, shards(): lax.all_gather(diag_rows, 'swath', axis=0, tiled=True)  50.5 us
    all_gather x1, waiting for transfers between devices, shards(): shard_rows = lax.all_gather(gram_input, 'swath', axis=0, tiled=True)  35.5 us
    another operation x42, matrix products, tri_solve(): lax.linalg.triangular_solve(factor, right, left_side=True, lower=True)  35 us
    ppermute x11, starting transfers between devices, passed_along(): return lax.ppermute(block, axis, route)  31.4 us
  transfers between devices with their start and end apart: 18, of which 11 were waited for; matrix products, arithmetic and copies ran while one was open for 66% of the time, Pallas kernels for 0%

commit v1 on v0

--- a/solution.py
+++ b/solution.py
@@ -53,7 +53,14 @@
     ahead_blocks = compact(scaled, live & (target == my_time + 1), slot_count)
     incoming, previous = passed_along((ahead_blocks, process), "tm", 1)
     gram_input = jnp.concatenate([own_blocks, incoming], axis=0).reshape(-1, order_size)
-    shard_rows = lax.all_gather(gram_input, "swath", axis=0, tiled=True)
+    ring = [gram_input]
+    for hop in range(3):
+        ring.append(lax.ppermute(ring[-1], "swath", [(dev, (dev + 1) % 4) for dev in range(4)]))
+    shard_rows = jnp.roll(
+        jnp.concatenate(ring[::-1], axis=0),
+        (lax.axis_index("swath") + 1) * ring[0].shape[0],
+        axis=0,
+    )
     columns = lax.dynamic_slice_in_dim(shard_rows, row_start, row_count, 1)
     gram = lax.dot_general(
         columns, shard_rows, (((0,), (0,)), ((), ())), preferred_element_type=jnp.float32

time: 894 us -> 837 us (0.936)
  the two profiles are of different devices: /device:TPU:16 before, /device:TPU:48 now
where the time goes in v1:
time: 837 us; the launch traced here: 832 us
  other arithmetic  496 us (59%)
  waiting for transfers between devices  129 us (15%)
  matrix products  75.9 us (9%)
  local copies, waits for them, and re-layouts  65.3 us (8%)
  starting transfers between devices  42.5 us (5%)
  between operations  23.6 us (3%)
    another operation x19, other arithmetic, tri_solve(): lax.linalg.triangular_solve(factor, right, left_side=True, lower=True)  248 us
    another operation x45, other arithmetic, shards(): factor = jnp.linalg.cholesky(full_diag)  238 us
    another operation x79, local copies, waits for them, and re-layouts, tri_solve(): lax.linalg.triangular_solve(factor, right, left_side=True, lower=True)  56.5 us
    all_gather x3, waiting for transfers between devices, shards(): lax.all_gather(diag_rows, 'swath', axis=0, tiled=True)  55.8 us
    another operation x42, matrix products, tri_solve(): lax.linalg.triangular_solve(factor, right, left_side=True, lower=True)  45.5 us
    ppermute x11, waiting for transfers between devices, passed_along(): return lax.ppermute(block, axis, route)  39.5 us
    ppermute x11, starting transfers between devices, passed_along(): return lax.ppermute(block, axis, route)  34.2 us
    ppermute x3, waiting for transfers between devices, shards(): lax.ppermute(ring[-1], 'swath', [(dev, (dev + 1) % 4) for dev in range(4)])  33.3 us
  transfers between devices with their start and end apart: 20, of which 9 were waited for; matrix products, arithmetic and copies ran while one was open for 74% of the time, Pallas kernels for 0%

profile of v1, /device:TPU:48, one launch (start us, length us, event | category | flops | bytes accessed | tf_op | source)
XLA Modules:
  0.0 832.0 jit_solution(7356956746891819887)
XLA Ops:
  17.1 4.4 collective-permute-done.1
  21.6 3.4 collective-permute-start.2
  25.0 11.8 %collective-permute-done.2 = bf16[512,512]{1,0:T(8,128)(2,1)S(1)} collective-permute-done((bf16[512,512]{1,0:T(8,128)(2,1)S(1)}, bf16[512,512]{1,0:T(8,128)(2,1)S(1)}, u32[]{:S(2)}, u32[]{:S(2)}) %collective-permute-start.2) | collective-permute-done | bytes 524320 | tf_op jit(solution)/shard_map/ppermute | solution.py:58
  36.9 2.2 collective-permute-start.3
  39.0 12.1 %collective-permute-done.3 = bf16[512,512]{1,0:T(8,128)(2,1)S(1)} collective-permute-done((bf16[512,512]{1,0:T(8,128)(2,1)S(1)}, bf16[512,512]{1,0:T(8,128)(2,1)S(1)}, u32[]{:S(2)}, u32[]{:S(2)}) %collective-permute-start.3) | collective-permute-done | bytes 524320 | tf_op jit(solution)/shard_map/ppermute | solution.py:58
  55.2 9.4 %collective-permute-done.4 = bf16[512,512]{1,0:T(8,128)(2,1)S(1)} collective-permute-done((bf16[512,512]{1,0:T(8,128)(2,1)S(1)}, bf16[512,512]{1,0:T(8,128)(2,1)S(1)}, u32[]{:S(2)}, u32[]{:S(2)}) %collective-permute-start.4) | collective-permute-done | bytes 524320 | tf_op jit(solution)/shard_map/ppermute | solution.py:58
  68.2 36.1 %all-gather.8.cloned.1.call-done = f32[512,512]{0,1:T(8,128)} async-done(((f32[128,512]{0,1:T(8,128)}), f32[512,512]{0,1:T(8,128)}) %all-gather.8.cloned.1.call-update) | async-done | bytes 1048592 | tf_op jit(solution)/shard_map/all_gather | solution.py:76
  107.3 11.7 %cholesky.374 = f32[128,128]{1,0:T(8,128)S(1)} custom-call(f32[128,128]{1,0:T(8,128)S(1)} %cholesky.586), custom_call_target="Cholesky" | custom-call | tf_op jit(solution)/shard_map/jit(cholesky)/cholesky | solution.py:79
  119.2 9.8 %custom-call.34 = f32[1,128,128]{1,2,0:T(8,128)S(1)} custom-call(f32[1,128,128]{2,1,0:T(8,128)S(1)} %get-tuple-element.152), custom_call_target="InvertDiagBlocksLowerTriangular" | custom-call | tf_op jit(solution)/shard_map/jit(cholesky)/cholesky | solution.py:79
  129.6 11.7 %cholesky.393 = f32[128,128]{1,0:T(8,128)S(1)} custom-call(f32[128,128]{1,0:T(8,128)S(1)} %cholesky.590), custom_call_target="Cholesky" | custom-call | tf_op jit(solution)/shard_map/jit(cholesky)/cholesky | solution.py:79
  142.7 10.0 %custom-call.35 = f32[1,128,128]{1,2,0:T(8,128)S(1)} custom-call(f32[1,128,128]{2,1,0:T(8,128)S(1)} %get-tuple-element.149), custom_call_target="InvertDiagBlocksLowerTriangular" | custom-call | tf_op jit(solution)/shard_map/jit(cholesky)/cholesky | solution.py:79
  153.3 11.7 %cholesky.414 = f32[128,128]{1,0:T(8,128)S(1)} custom-call(f32[128,128]{1,0:T(8,128)S(1)} %cholesky.595), custom_call_target="Cholesky" | custom-call | tf_op jit(solution)/shard_map/jit(cholesky)/cholesky | solution.py:79
  165.7 9.8 %custom-call.36 = f32[1,128,128]{1,2,0:T(8,128)S(1)} custom-call(f32[1,128,128]{2,1,0:T(8,128)S(1)} %get-tuple-element.146), custom_call_target="InvertDiagBlocksLowerTriangular" | custom-call | tf_op jit(solution)/shard_map/jit(cholesky)/cholesky | solution.py:79
  176.1 11.7 %cholesky.431 = f32[128,128]{1,0:T(8,128)S(1)} custom-call(f32[128,128]{1,0:T(8,128)S(1)} %convolution_subtract_fusion.14), custom_call_target="Cholesky" | custom-call | tf_op jit(solution)/shard_map/jit(cholesky)/cholesky | solution.py:79
  193.6 7.9 while.12
  201.4 39.3 %custom-call.37 = f32[4,128,128]{1,2,0:T(8,128)S(1)} custom-call(f32[4,128,128]{2,1,0:T(8,128)S(1)} %get-tuple-element.47), custom_call_target="InvertDiagBlocksLowerTriangular" | custom-call | tf_op jit(solution)/shard_map/triangular_solve/custom-call.3 | solution.py:16
  246.5 2.5 convolution_subtract_fusion.5
  249.6 2.5 fusion.104
  252.1 2.4 collective-permute-start.5
  256.6 10.4 %while.13 = (s32[]{:T(128)}, f32[512,512]{1,0:T(8,128)S(1)}, s32[4,2]{0,1:T(2,128)S(1)}, f32[4,128,128]{2,1,0:T(8,128)}, s32[]{:T(128)}) while((s32[]{:T(128)}, f32[512,512]{1,0:T(8,128)S(1)}, s32[4,2]{0,1:T(2,128)S(1)}, f32[4,128,128]{2,1,0:T(8,128)}, s32[]{:T(128)}) %tuple.155), condition=%wide.while_cond.clone, body=%wide.while_body.clone.sunk | while | flops 2 | bytes 132705 | solution.py:16
  267.0 40.8 %custom-call.38 = f32[4,128,128]{1,2,0:T(8,128)} custom-call(f32[4,128,128]{2,1,0:T(8,128)} %get-tuple-element.48), custom_call_target="InvertDiagBlocksLowerTriangular" | custom-call | tf_op jit(solution)/shard_map/triangular_solve/custom-call.3 | solution.py:16
  314.4 3.5 subtract_subtract_fusion.1
  317.9 3.2 collective-permute-start.7
  321.1 12.3 %collective-permute-done.7 = f32[512,512]{1,0:T(8,128)S(1)} collective-permute-done((f32[512,512]{1,0:T(8,128)S(1)}, f32[512,512]{1,0:T(8,128)S(1)}, u32[]{:S(2)}, u32[]{:S(2)}) %collective-permute-start.7) | collective-permute-done | bytes 1048608 | tf_op jit(solution)/shard_map/ppermute | solution.py:12
  335.1 15.2 %all-gather.10.cloned.1.call-done = f32[512,512]{0,1:T(8,128)} async-done(((f32[128,512]{0,1:T(8,128)}), f32[512,512]{0,1:T(8,128)}) %all-gather.10.cloned.1.call-update) | async-done | bytes 1048592 | tf_op jit(solution)/shard_map/all_gather | solution.py:76
  353.3 11.7 %cholesky.446 = f32[128,128]{1,0:T(8,128)S(1)} custom-call(f32[128,128]{1,0:T(8,128)S(1)} %cholesky.599), custom_call_target="Cholesky" | custom-call | tf_op jit(solution)/shard_map/jit(cholesky)/cholesky | solution.py:79
  365.2 9.8 %custom-call.39 = f32[1,128,128]{1,2,0:T(8,128)S(1)} custom-call(f32[1,128,128]{2,1,0:T(8,128)S(1)} %get-tuple-element.142), custom_call_target="InvertDiagBlocksLowerTriangular" | custom-call | tf_op jit(solution)/shard_map/jit(cholesky)/cholesky | solution.py:79
  375.7 11.7 %cholesky.465 = f32[128,128]{1,0:T(8,128)S(1)} custom-call(f32[128,128]{1,0:T(8,128)S(1)} %cholesky.603), custom_call_target="Cholesky" | custom-call | tf_op jit(solution)/shard_map/jit(cholesky)/cholesky | solution.py:79
  388.7 10.0 %custom-call.40 = f32[1,128,128]{1,2,0:T(8,128)S(1)} custom-call(f32[1,128,128]{2,1,0:T(8,128)S(1)} %get-tuple-element.139), custom_call_target="InvertDiagBlocksLowerTriangular" | custom-call | tf_op jit(solution)/shard_map/jit(cholesky)/cholesky | solution.py:79
  399.4 11.7 %cholesky.486 = f32[128,128]{1,0:T(8,128)S(1)} custom-call(f32[128,128]{1,0:T(8,128)S(1)} %cholesky.608), custom_call_target="Cholesky" | custom-call | tf_op jit(solution)/shard_map/jit(cholesky)/cholesky | solution.py:79
  411.8 9.8 %custom-call.41 = f32[1,128,128]{1,2,0:T(8,128)S(1)} custom-call(f32[1,128,128]{2,1,0:T(8,128)S(1)} %get-tuple-element.136), custom_call_target="InvertDiagBlocksLowerTriangular" | custom-call | tf_op jit(solution)/shard_map/jit(cholesky)/cholesky | solution.py:79
  422.2 11.7 %cholesky.503 = f32[128,128]{1,0:T(8,128)S(1)} custom-call(f32[128,128]{1,0:T(8,128)S(1)} %convolution_subtract_fusion.13), custom_call_target="Cholesky" | custom-call | tf_op jit(solution)/shard_map/jit(cholesky)/cholesky | solution.py:79
  437.7 3.3 collective-permute-start.9
  441.0 7.9 while.14
  448.9 39.9 %custom-call.42 = f32[4,128,128]{1,2,0:T(8,128)} custom-call(f32[4,128,128]{2,1,0:T(8,128)S(1)} %get-tuple-element.49), custom_call_target="InvertDiagBlocksLowerTriangular" | custom-call | tf_op jit(solution)/shard_map/triangular_solve/custom-call.3 | solution.py:16
  496.0 2.5 fusion.102
  498.5 2.7 collective-permute-start.8
  503.3 10.6 %while.15 = (s32[]{:T(128)}, f32[512,512]{1,0:T(8,128)S(1)}, s32[4,2]{0,1:T(2,128)S(1)}, f32[4,128,128]{2,1,0:T(8,128)}, s32[]{:T(128)}) while((s32[]{:T(128)}, f32[512,512]{1,0:T(8,128)S(1)}, s32[4,2]{0,1:T(2,128)S(1)}, f32[4,128,128]{2,1,0:T(8,128)}, s32[]{:T(128)}) %tuple.157), condition=%wide.while_cond.clone.2, body=%wide.while_body.clone.2.sunk | while | flops 2 | bytes 132705 | solution.py:16
  504.0 2.0 bitcast_dynamic-update-slice_fusion.15
  506.6 2.0 bitcast_dynamic-update-slice_fusion.15
  509.3 2.0 bitcast_dynamic-update-slice_fusion.15
  511.9 2.0 bitcast_dynamic-update-slice_fusion.15
  513.9 40.8 %custom-call.43 = f32[4,128,128]{1,2,0:T(8,128)} custom-call(f32[4,128,128]{2,1,0:T(8,128)} %get-tuple-element.50), custom_call_target="InvertDiagBlocksLowerTriangular" | custom-call | tf_op jit(solution)/shard_map/triangular_solve/custom-call.3 | solution.py:16
  563.0 3.5 subtract_subtract_fusion
  566.5 3.6 collective-permute-start.10
  570.1 22.8 %collective-permute-done.10 = f32[512,512]{1,0:T(8,128)S(1)} collective-permute-done((f32[512,512]{1,0:T(8,128)S(1)}, f32[512,512]{1,0:T(8,128)S(1)}, u32[]{:S(2)}, u32[]{:S(2)}) %collective-permute-start.10) | collective-permute-done | bytes 1048608 | tf_op jit(solution)/shard_map/ppermute | solution.py:12
  594.4 4.5 all-gather.14.cloned.1.call-done
  601.9 11.7 %cholesky.518 = f32[128,128]{1,0:T(8,128)S(1)} custom-call(f32[128,128]{1,0:T(8,128)S(1)} %cholesky.612), custom_call_target="Cholesky" | custom-call | tf_op jit(solution)/shard_map/jit(cholesky)/cholesky | solution.py:79
  613.8 9.8 %custom-call.44 = f32[1,128,128]{1,2,0:T(8,128)S(1)} custom-call(f32[1,128,128]{2,1,0:T(8,128)S(1)} %get-tuple-element.132), custom_call_target="InvertDiagBlocksLowerTriangular" | custom-call | tf_op jit(solution)/shard_map/jit(cholesky)/cholesky | solution.py:79
  624.3 11.7 %cholesky.537 = f32[128,128]{1,0:T(8,128)S(1)} custom-call(f32[128,128]{1,0:T(8,128)S(1)} %cholesky.616), custom_call_target="Cholesky" | custom-call | tf_op jit(solution)/shard_map/jit(cholesky)/cholesky | solution.py:79
  637.4 10.2 %custom-call.45 = f32[1,128,128]{1,2,0:T(8,128)S(1)} custom-call(f32[1,128,128]{2,1,0:T(8,128)S(1)} %get-tuple-element.129), custom_call_target="InvertDiagBlocksLowerTriangular" | custom-call | tf_op jit(solution)/shard_map/jit(cholesky)/cholesky | solution.py:79
  648.2 11.7 %cholesky.558 = f32[128,128]{1,0:T(8,128)S(1)} custom-call(f32[128,128]{1,0:T(8,128)S(1)} %cholesky.621), custom_call_target="Cholesky" | custom-call | tf_op jit(solution)/shard_map/jit(cholesky)/cholesky | solution.py:79
  660.7 9.8 %custom-call.46 = f32[1,128,128]{1,2,0:T(8,128)S(1)} custom-call(f32[1,128,128]{2,1,0:T(8,128)S(1)} %get-tuple-element.126), custom_call_target="InvertDiagBlocksLowerTriangular" | custom-call | tf_op jit(solution)/shard_map/jit(cholesky)/cholesky | solution.py:79
  671.1 11.9 %cholesky.575 = f32[128,128]{1,0:T(8,128)S(1)} custom-call(f32[128,128]{1,0:T(8,128)S(1)} %convolution_subtract_fusion.12), custom_call_target="Cholesky" | custom-call | tf_op jit(solution)/shard_map/jit(cholesky)/cholesky | solution.py:79
  686.5 4.2 collective-permute-start.12
  690.7 7.8 while.16
  698.6 39.9 %custom-call.47 = f32[4,128,128]{1,2,0:T(8,128)} custom-call(f32[4,128,128]{2,1,0:T(8,128)S(1)} %get-tuple-element.51), custom_call_target="InvertDiagBlocksLowerTriangular" | custom-call | tf_op jit(solution)/shard_map/triangular_solve/custom-call.3 | solution.py:16
  745.7 2.4 collective-permute-start.13
  748.1 2.5 fusion.100
  750.6 6.6 collective-permute-start.11
  759.4 10.1 %while.17 = (s32[]{:T(128)}, f32[512,512]{1,0:T(8,128)S(1)}, s32[4,2]{0,1:T(2,128)S(1)}, f32[4,128,128]{2,1,0:T(8,128)}, s32[]{:T(128)}) while((s32[]{:T(128)}, f32[512,512]{1,0:T(8,128)S(1)}, s32[4,2]{0,1:T(2,128)S(1)}, f32[4,128,128]{2,1,0:T(8,128)}, s32[]{:T(128)}) %tuple.159), condition=%wide.while_cond.clone.4, body=%wide.while_body.clone.4.sunk | while | flops 2 | bytes 132705 | solution.py:16
  769.5 40.8 %custom-call.48 = f32[4,128,128]{1,2,0:T(8,128)} custom-call(f32[4,128,128]{2,1,0:T(8,128)} %get-tuple-element.52), custom_call_target="InvertDiagBlocksLowerTriangular" | custom-call | tf_op jit(solution)/shard_map/triangular_solve/custom-call.3 | solution.py:16
  818.6 2.8 subtract_bitcast_fusion
  822.2 2.7 fusion.2
  (267 shorter events, 144.0 us)
Async XLA Ops:
  7.2 45.9 %copy-start.6 = (bf16[1,128,512]{2,1,0:T(8,128)(2,1)S(1)}, bf16[1,128,512]{2,1,0:T(8,128)(2,1)}, u32[]{:S(2)}) copy-start(bf16[1,128,512]{2,1,0:T(8,128)(2,1)} %param.11) | copy-start | bytes 393220
  7.2 97.1 %all-gather.8.cloned.1.call-start = ((), (), s32[]{:S(2)}) async-start(), calls=%async_computation | async-start | bytes 1310720 | tf_op jit(solution)/shard_map/all_gather | solution.py:76
  13.9 7.7 collective-permute-start.1
  21.6 15.2 %collective-permute-start.2 = (bf16[512,512]{1,0:T(8,128)(2,1)S(1)}, bf16[512,512]{1,0:T(8,128)(2,1)S(1)}, u32[]{:S(2)}, u32[]{:S(2)}) collective-permute-start(bf16[512,512]{1,0:T(8,128)(2,1)S(1)} %bitcast.250), channel_id=1, source_target_pairs={{0,1},{1,2},{2,3},{3,0},{4,5},{5,6},{6,7},{7,4},{8,9},{9,10},{10,1... | collective-permute-start | bytes 1572872 | tf_op jit(solution)/shard_map/ppermute | solution.py:58
  36.9 14.3 %collective-permute-start.3 = (bf16[512,512]{1,0:T(8,128)(2,1)S(1)}, bf16[512,512]{1,0:T(8,128)(2,1)S(1)}, u32[]{:S(2)}, u32[]{:S(2)}) collective-permute-start(bf16[512,512]{1,0:T(8,128)(2,1)S(1)} %collective-permute-done.2), channel_id=1, source_target_pairs={{0,1},{1,2},{2,3},{3,0},{4,5},{5,6},{6,7},{7,4},{8,9},{9,10},{10,1... | collective-permute-start | bytes 1572872 | tf_op jit(solution)/shard_map/ppermute | solution.py:58
  51.2 13.4 %collective-permute-start.4 = (bf16[512,512]{1,0:T(8,128)(2,1)S(1)}, bf16[512,512]{1,0:T(8,128)(2,1)S(1)}, u32[]{:S(2)}, u32[]{:S(2)}) collective-permute-start(bf16[512,512]{1,0:T(8,128)(2,1)S(1)} %collective-permute-done.3), channel_id=1, source_target_pairs={{0,1},{1,2},{2,3},{3,0},{4,5},{5,6},{6,7},{7,4},{8,9},{9,10},{10,1... | collective-permute-start | bytes 1572872 | tf_op jit(solution)/shard_map/ppermute | solution.py:58
  53.2 11.7 %collective-permute-start = (bf16[1,128,512]{1,2,0:T(8,128)(2,1)S(1)}, bf16[1,128,512]{1,2,0:T(8,128)(2,1)S(1)}, u32[]{:S(2)}, u32[]{:S(2)}) collective-permute-start(bf16[1,128,512]{1,2,0:T(8,128)(2,1)S(1)} %copy.20), channel_id=1, source_target_pairs={{0,4},{4,8},{8,12},{12,16},{16,20},{20,24},{24,28},{28,32},{32,36}... | collective-permute-start | bytes 393224 | tf_op jit(solution)/shard_map/ppermute | solution.py:12
  55.2 9.7 %copy-start.7 = (f32[1,128]{1,0:T(1,128)S(1)}, f32[1,128]{1,0:T(1,128)}, u32[]{:S(2)}) copy-start(f32[1,128]{1,0:T(1,128)} %param.12) | copy-start | bytes 1540
  66.8 173.9 %all-gather.18.cloned.1.call-start = ((), (), s32[]{:S(2)}) async-start(), calls=%async_computation.5 | async-start | bytes 1310720 | tf_op jit(solution)/shard_map/all_gather | solution.py:77
  67.6 282.6 %all-gather.10.cloned.1.call-start = ((), (), s32[]{:S(2)}) async-start(), calls=%async_computation.1 | async-start | bytes 1310720 | tf_op jit(solution)/shard_map/all_gather | solution.py:76
  191.6 62.9 %collective-permute-start.6 = (f32[512,512]{1,0:T(8,128)S(1)}, f32[512,512]{1,0:T(8,128)}, u32[]{:S(2)}, u32[]{:S(2)}) collective-permute-start(f32[512,512]{1,0:T(8,128)S(1)} %get-tuple-element.110), channel_id=1, source_target_pairs={{4,0},{8,4},{12,8},{16,12},{20,16},{24,20},{28,24},{32,28},{36,32}... | collective-permute-start | bytes 3145736 | tf_op jit(solution)/shard_map/ppermute | solution.py:12
  246.5 61.2 %copy-start.2 = (f32[1,512,512]{1,2,0:T(8,128)S(1)}, f32[1,512,512]{1,2,0:T(8,128)}, u32[]{:S(2)}) copy-start(f32[1,512,512]{1,2,0:T(8,128)} %all-gather.18.cloned.1.call-done) | copy-start | bytes 3145732
  252.1 62.3 %collective-permute-start.5 = (f32[128,512]{0,1:T(8,128)}, f32[128,512]{0,1:T(8,128)}, u32[]{:S(2)}, u32[]{:S(2)}) collective-permute-start(f32[128,512]{0,1:T(8,128)} %fusion.104), channel_id=1, source_target_pairs={{0,4},{4,8},{8,12},{12,16},{16,20},{20,24},{24,28},{28,32},{32,36}... | collective-permute-start | bytes 786440 | tf_op jit(solution)/shard_map/ppermute | solution.py:12
  267.0 47.4 %copy-start.5 = (f32[128,512]{0,1:T(8,128)S(1)}, f32[128,512]{0,1:T(8,128)}, u32[]{:S(2)}) copy-start(f32[128,512]{0,1:T(8,128)} %fusion.72) | copy-start | bytes 786436
  317.9 171.0 %all-gather.12.cloned.1.call-start = ((), (), s32[]{:S(2)}) async-start(), calls=%async_computation.2 | async-start | bytes 1310720 | tf_op jit(solution)/shard_map/all_gather | solution.py:77
  317.9 15.5 %collective-permute-start.7 = (f32[512,512]{1,0:T(8,128)S(1)}, f32[512,512]{1,0:T(8,128)S(1)}, u32[]{:S(2)}, u32[]{:S(2)}) collective-permute-start(f32[512,512]{1,0:T(8,128)S(1)} %pad_maximum_fusion), channel_id=1, source_target_pairs={{4,0},{8,4},{12,8},{16,12},{20,16},{24,20},{28,24},{32,28},{36,32}... | collective-permute-start | bytes 3145736 | tf_op jit(solution)/shard_map/ppermute | solution.py:12
  334.9 264.0 %all-gather.14.cloned.1.call-start = ((), (), s32[]{:S(2)}) async-start(), calls=%async_computation.3 | async-start | bytes 1310720 | tf_op jit(solution)/shard_map/all_gather | solution.py:76
  437.7 63.5 %collective-permute-start.9 = (f32[512,512]{1,0:T(8,128)S(1)}, f32[512,512]{1,0:T(8,128)}, u32[]{:S(2)}, u32[]{:S(2)}) collective-permute-start(f32[512,512]{1,0:T(8,128)S(1)} %get-tuple-element.108), channel_id=1, source_target_pairs={{8,0},{12,4},{16,8},{20,12},{24,16},{28,20},{32,24},{36,28},{40,32... | collective-permute-start | bytes 3145736 | tf_op jit(solution)/shard_map/ppermute | solution.py:12
  488.8 5.8 copy-start.1
  498.5 64.5 %collective-permute-start.8 = (f32[128,512]{0,1:T(8,128)}, f32[128,512]{0,1:T(8,128)}, u32[]{:S(2)}, u32[]{:S(2)}) collective-permute-start(f32[128,512]{0,1:T(8,128)} %fusion.102), channel_id=1, source_target_pairs={{0,8},{4,12},{8,16},{12,20},{16,24},{20,28},{24,32},{28,36},{32,40... | collective-permute-start | bytes 786440 | tf_op jit(solution)/shard_map/ppermute | solution.py:12
  513.9 49.1 %copy-start.4 = (f32[128,512]{0,1:T(8,128)S(1)}, f32[128,512]{0,1:T(8,128)}, u32[]{:S(2)}) copy-start(f32[128,512]{0,1:T(8,128)} %subtract_subtract_fusion.1) | copy-start | bytes 786436
  566.5 172.0 %all-gather.16.cloned.1.call-start = ((), (), s32[]{:S(2)}) async-start(), calls=%async_computation.4 | async-start | bytes 1310720 | tf_op jit(solution)/shard_map/all_gather | solution.py:77
  566.5 26.3 %collective-permute-start.10 = (f32[512,512]{1,0:T(8,128)S(1)}, f32[512,512]{1,0:T(8,128)S(1)}, u32[]{:S(2)}, u32[]{:S(2)}) collective-permute-start(f32[512,512]{1,0:T(8,128)S(1)} %pad_maximum_fusion.2), channel_id=1, source_target_pairs={{8,0},{12,4},{16,8},{20,12},{24,16},{28,20},{32,24},{36,28},{40,32... | collective-permute-start | bytes 3145736 | tf_op jit(solution)/shard_map/ppermute | solution.py:12
  686.5 70.8 %collective-permute-start.12 = (f32[512,512]{1,0:T(8,128)S(1)}, f32[512,512]{1,0:T(8,128)}, u32[]{:S(2)}, u32[]{:S(2)}) collective-permute-start(f32[512,512]{1,0:T(8,128)S(1)} %get-tuple-element.106), channel_id=1, source_target_pairs={{16,0},{20,4},{24,8},{28,12},{32,16},{36,20},{40,24},{44,28},{48,3... | collective-permute-start | bytes 3145736 | tf_op jit(solution)/shard_map/ppermute | solution.py:12
  738.5 5.8 copy-start
  745.7 76.5 %collective-permute-start.13 = (f32[512,512]{1,0:T(8,128)S(1)}, f32[512,512]{1,0:T(8,128)}, u32[]{:S(2)}, u32[]{:S(2)}) collective-permute-start(f32[512,512]{1,0:T(8,128)S(1)} %pad_maximum_fusion.4), channel_id=1, source_target_pairs={{16,0},{20,4},{24,8},{28,12},{32,16},{36,20},{40,24},{44,28},{48,3... | collective-permute-start | bytes 3145736 | tf_op jit(solution)/shard_map/ppermute | solution.py:12
  750.6 67.9 %collective-permute-start.11 = (f32[128,512]{0,1:T(8,128)}, f32[128,512]{0,1:T(8,128)}, u32[]{:S(2)}, u32[]{:S(2)}) collective-permute-start(f32[128,512]{0,1:T(8,128)} %fusion.100), channel_id=1, source_target_pairs={{0,16},{4,20},{8,24},{12,28},{16,32},{20,36},{24,40},{28,44},{32,4... | collective-permute-start | bytes 786440 | tf_op jit(solution)/shard_map/ppermute | solution.py:12
  769.5 49.1 %copy-start.3 = (f32[128,512]{0,1:T(8,128)S(1)}, f32[128,512]{0,1:T(8,128)}, u32[]{:S(2)}) copy-start(f32[128,512]{0,1:T(8,128)} %subtract_subtract_fusion) | copy-start | bytes 786436
Sparse Core Ops, SparseCore 0:
  67.0 37.2 all-gather.7
  106.9 31.9 all-gather.17
  318.0 32.2 all-gather.9
  352.8 30.7 all-gather.11
  566.6 32.2 all-gather.13
  601.4 30.7 all-gather.15
